TPU v7x, 32 devices: a whole 2x2x4 slice. The times are simulated.
32 devices in a mesh: ens: 2 (over x), lat: 16 (over z, y, core).
Axes of the slice: x: 2, y: 2, z: 4, core: 2. Of those that a mesh axis runs over, the one named last changes fastest.
Arguments:
- cot_next: float32 [6, 10, 64, 4320], P('ens', None, 'lat'), parts along dimension 0, may hold values from -6 to 6
- cot_surface: float32 [128, 4320], P(('ens', 'lat')), parts along dimension 0, may hold values from -4 to 4
- stencil: float32 [5, 64, 4320], P(None, 'lat'), may hold values from 0.1 to 0.5
- mix: float32 [9, 64, 4320], P(None, 'lat'), may hold values from 0.1 to 10
- weights: float32 [3, 10], replicated, may hold values from 0.2 to 1
- depth: float32 [64, 4320], P('lat'), may hold values from 0.5 to 6
- surface_mass: float32 [64, 4320], P('lat'), may hold values from 0.005 to 0.05
- ocean: int32 [64, 4320], P('lat'), may hold values 0 or 1
- fold_sign: int32 [3, 10], replicated, may hold values from 0 to 1
Outputs:
- cot_state: float32 [6, 10, 64, 4320], P('ens', None, 'lat'), parts along dimension 0
- surface_adjoint: float32 [128, 4320], P(('ens', 'lat')), parts along dimension 0
There are 2 independent parts, one for each index of `ens`. A program takes and returns all parts, laid end to end along the dimension named above; an argument that names none is the same for every part. Nothing has to cross between parts.
All inputs are finite; a program needn't handle non-finite values. No bound on the sum of `ocean` on one device may be relied on, other than what follows from the above.
Results may differ from a plain program's by a relative error of at most 0.0003.
Values sent between devices are 32-bit elements; how exact they have to be, the bound alone decides.
A program may use at most 128 MiB of HBM per device.

v0:
```python
import jax
import jax.numpy as jnp
from jax import lax
from jax.sharding import PartitionSpec as P

ITERS = 10


def padded(x, sides, width):
    for axis, dim in sides:
        size, length = (lax.axis_size(axis), x.shape[dim])
        up = [(i, (i + 1) % size) for i in range(size - 1)]
        down = [(j, i) for i, j in up]
        last = lax.slice_in_dim(x, length - width, length, axis=dim)
        initial = lax.slice_in_dim(x, 0, width, axis=dim)
        before = lax.ppermute(last, axis, up)
        after = lax.ppermute(initial, axis, down)
        x = jnp.concatenate([before, x, after], axis=dim)
    return x


def passed_along(value, axis, steps):
    count = lax.axis_size(axis)
    initial, last = (max(0, -steps), min(count, count - steps))
    return lax.ppermute(value, axis, [(source, source + steps) for source in range(initial, last)])


def column_solve(rhs, mix):
    levels = rhs.shape[1]
    ratios = []
    reduced = []
    for level in range(levels):
        below = mix[level - 1] if level > 0 else 0.0
        above = mix[level] if level < levels - 1 else 0.0
        pivot = 1.0 + below + above
        source = rhs[:, level]
        if level > 0:
            pivot = pivot + below * ratios[-1]
            source = source + below * reduced[-1]
        ratios.append(-above / pivot)
        reduced.append(source / pivot)
    result = [reduced[-1]]
    for level in range(levels - 2, -1, -1):
        result.insert(0, reduced[level] - ratios[level] * result[0])
    return jnp.stack(result, axis=1)


def surface_apply(field, links):
    east_link, north_link, south_link, centre = links
    rimmed = padded(field, (("lat", 0),), 1)
    return (
        centre * field
        - east_link * jnp.roll(field, -1, 1)
        - jnp.roll(east_link, 1, 1) * jnp.roll(field, 1, 1)
        - north_link * rimmed[2:]
        - south_link * rimmed[:-2]
    )


def residual_norm(residual, scaled):
    return lax.psum(jnp.sum(residual * scaled), "lat")


def classic_solve(rhs, links):
    centre = links[3]
    surface = jnp.zeros_like(rhs)
    residual = rhs
    scaled = residual / centre
    direction = scaled
    norm_now = residual_norm(residual, scaled)
    for iteration in range(ITERS):
        applied = surface_apply(direction, links)
        step_size = norm_now / lax.psum(jnp.sum(direction * applied), "lat")
        surface = surface + step_size * direction
        if iteration < ITERS - 1:
            residual = residual - step_size * applied
            scaled = residual / centre
            norm_next = residual_norm(residual, scaled)
            direction = scaled + norm_next / norm_now * direction
            norm_now = norm_next
    return surface


def shards(cot_next, cot_surface, stencil, mix, weights, depth, surface_mass, ocean, fold_sign):
    wet_cells = ocean.astype(jnp.float32)
    coastal = padded(jnp.stack([depth, wet_cells]), (("lat", 1),), 1)
    depth_rows = coastal[0]
    wet_rows = coastal[1]
    north_all = 0.5 * (depth_rows[:-1] + depth_rows[1:]) * wet_rows[:-1] * wet_rows[1:]
    north_link = north_all[1:]
    south_link = north_all[:-1]
    east_link = 0.5 * (depth + jnp.roll(depth, -1, 1)) * wet_cells * jnp.roll(wet_cells, -1, 1)
    centre = surface_mass + east_link + jnp.roll(east_link, 1, 1) + north_link + south_link
    links = (east_link, north_link, south_link, centre)
    lift_weights = weights[:, :, None, None]
    rhs = wet_cells * cot_surface
    surface = classic_solve(rhs, links)
    mixed = column_solve(cot_next + lift_weights * (depth * surface)[None, None], mix)
    damped = wet_cells * mixed
    centre_c, west_c, east_c, south_c, north_c = (
        stencil[0],
        stencil[1],
        stencil[2],
        stencil[3],
        stencil[4],
    )
    total = centre_c * damped + jnp.roll(west_c * damped, -1, -1) + jnp.roll(east_c * damped, 1, -1)
    lifted = south_c * damped
    lowered = north_c * damped
    from_above = passed_along(lifted[:, :, :1], "lat", -1)
    from_below = passed_along(lowered[:, :, -1:], "lat", 1)
    vertical = jnp.concatenate([lifted[:, :, 1:], from_above], axis=2) + jnp.concatenate(
        [from_below, lowered[:, :, :-1]], axis=2
    )
    total = total + vertical
    fold_factor = (2 * fold_sign - 1).astype(jnp.float32)
    folded = fold_factor[:, :, None] * (north_c[-1, ::-1] * damped[:, :, -1, ::-1])
    at_top = lax.axis_index("lat") == lax.axis_size("lat") - 1
    total = total.at[:, :, -1, :].add(jnp.where(at_top, folded, 0.0))
    return (total, surface)


def solution(mesh):
    in_specs = (
        P("ens", None, "lat", None),
        P(("ens", "lat"), None),
        P(None, "lat", None),
        P(None, "lat", None),
        P(),
        P("lat", None),
        P("lat", None),
        P("lat", None),
        P(),
    )
    out_specs = (P("ens", None, "lat", None), P(("ens", "lat"), None))
    return jax.shard_map(shards, mesh=mesh, in_specs=in_specs, out_specs=out_specs, check_vma=False)
```

profile of v0, /device:TPU:11, one launch (start us, length us, event | category | flops | bytes accessed | tf_op | source)
XLA Modules:
  0.0 767.0 jit_solution(15735047112464266464)
XLA Ops:
  2.7 3.7 collective-permute-start
  15.1 3.6 collective-permute-start.3
  20.8 3.1 collective-permute-done.2
  24.7 23.0 %all-reduce = (f32[]{:T(128)}, f32[]{:T(128)}) all-reduce(f32[]{:T(128)} %get-tuple-element.17, f32[]{:T(128)} %get-tuple-element.16), channel_id=1, replica_groups=mesh['ens'=2,'lat'=16] {'lat'}, use_global_device_ids=true, to_apply=%region_1.2 | all-reduce | flops 2 | bytes 16 | tf_op jit(solution)/shard_map/psum | solution.py:61
  49.6 29.8 %psum.142 = f32[]{:T(128)} all-reduce(f32[]{:T(128)} %get-tuple-element.90), channel_id=1, replica_groups=mesh['ens'=2,'lat'=16] {'lat'}, use_global_device_ids=true, to_apply=%region_5.6 | all-reduce | flops 1 | bytes 8 | tf_op jit(solution)/shard_map/psum | solution.py:61
  82.8 2.6 collective-permute-start.4
  85.5 2.4 collective-permute-done.4
  88.7 28.1 %psum.143 = f32[]{:T(128)} all-reduce(f32[]{:T(128)} %get-tuple-element.88), channel_id=1, replica_groups=mesh['ens'=2,'lat'=16] {'lat'}, use_global_device_ids=true, to_apply=%region_7.8 | all-reduce | flops 1 | bytes 8 | tf_op jit(solution)/shard_map/psum | solution.py:73
  118.7 32.0 %psum.144 = f32[]{:T(128)} all-reduce(f32[]{:T(128)} %get-tuple-element.85), channel_id=1, replica_groups=mesh['ens'=2,'lat'=16] {'lat'}, use_global_device_ids=true, to_apply=%region_9.10 | all-reduce | flops 1 | bytes 8 | tf_op jit(solution)/shard_map/psum | solution.py:61
  154.2 2.6 collective-permute-start.6
  156.8 2.4 collective-permute-done.6
  160.0 28.1 %psum.145 = f32[]{:T(128)} all-reduce(f32[]{:T(128)} %get-tuple-element.83), channel_id=1, replica_groups=mesh['ens'=2,'lat'=16] {'lat'}, use_global_device_ids=true, to_apply=%region_11.12 | all-reduce | flops 1 | bytes 8 | tf_op jit(solution)/shard_map/psum | solution.py:73
  190.0 32.0 %psum.146 = f32[]{:T(128)} all-reduce(f32[]{:T(128)} %get-tuple-element.80), channel_id=1, replica_groups=mesh['ens'=2,'lat'=16] {'lat'}, use_global_device_ids=true, to_apply=%region_13.14 | all-reduce | flops 1 | bytes 8 | tf_op jit(solution)/shard_map/psum | solution.py:61
  225.5 2.6 collective-permute-start.8
  228.1 2.4 collective-permute-done.8
  231.3 28.1 %psum.147 = f32[]{:T(128)} all-reduce(f32[]{:T(128)} %get-tuple-element.78), channel_id=1, replica_groups=mesh['ens'=2,'lat'=16] {'lat'}, use_global_device_ids=true, to_apply=%region_15.16 | all-reduce | flops 1 | bytes 8 | tf_op jit(solution)/shard_map/psum | solution.py:73
  261.4 32.0 %psum.148 = f32[]{:T(128)} all-reduce(f32[]{:T(128)} %get-tuple-element.75), channel_id=1, replica_groups=mesh['ens'=2,'lat'=16] {'lat'}, use_global_device_ids=true, to_apply=%region_17.18 | all-reduce | flops 1 | bytes 8 | tf_op jit(solution)/shard_map/psum | solution.py:61
  296.8 2.6 collective-permute-start.10
  299.5 2.4 collective-permute-done.10
  302.7 28.1 %psum.149 = f32[]{:T(128)} all-reduce(f32[]{:T(128)} %get-tuple-element.73), channel_id=1, replica_groups=mesh['ens'=2,'lat'=16] {'lat'}, use_global_device_ids=true, to_apply=%region_19.20 | all-reduce | flops 1 | bytes 8 | tf_op jit(solution)/shard_map/psum | solution.py:73
  332.7 32.0 %psum.150 = f32[]{:T(128)} all-reduce(f32[]{:T(128)} %get-tuple-element.70), channel_id=1, replica_groups=mesh['ens'=2,'lat'=16] {'lat'}, use_global_device_ids=true, to_apply=%region_21.22 | all-reduce | flops 1 | bytes 8 | tf_op jit(solution)/shard_map/psum | solution.py:61
  368.1 2.6 collective-permute-start.12
  370.8 2.4 collective-permute-done.12
  374.0 28.1 %psum.151 = f32[]{:T(128)} all-reduce(f32[]{:T(128)} %get-tuple-element.68), channel_id=1, replica_groups=mesh['ens'=2,'lat'=16] {'lat'}, use_global_device_ids=true, to_apply=%region_23.24 | all-reduce | flops 1 | bytes 8 | tf_op jit(solution)/shard_map/psum | solution.py:73
  404.0 32.0 %psum.152 = f32[]{:T(128)} all-reduce(f32[]{:T(128)} %get-tuple-element.65), channel_id=1, replica_groups=mesh['ens'=2,'lat'=16] {'lat'}, use_global_device_ids=true, to_apply=%region_25.26 | all-reduce | flops 1 | bytes 8 | tf_op jit(solution)/shard_map/psum | solution.py:61
  439.5 2.6 collective-permute-start.14
  442.1 2.4 collective-permute-done.14
  445.3 28.1 %psum.153 = f32[]{:T(128)} all-reduce(f32[]{:T(128)} %get-tuple-element.63), channel_id=1, replica_groups=mesh['ens'=2,'lat'=16] {'lat'}, use_global_device_ids=true, to_apply=%region_27.28 | all-reduce | flops 1 | bytes 8 | tf_op jit(solution)/shard_map/psum | solution.py:73
  476.0 32.0 %psum.154 = f32[]{:T(128)} all-reduce(f32[]{:T(128)} %get-tuple-element.60), channel_id=1, replica_groups=mesh['ens'=2,'lat'=16] {'lat'}, use_global_device_ids=true, to_apply=%region_29.30 | all-reduce | flops 1 | bytes 8 | tf_op jit(solution)/shard_map/psum | solution.py:61
  511.5 2.6 collective-permute-start.16
  514.1 2.4 collective-permute-done.16
  518.0 28.1 %psum.155 = f32[]{:T(128)} all-reduce(f32[]{:T(128)} %get-tuple-element.58), channel_id=1, replica_groups=mesh['ens'=2,'lat'=16] {'lat'}, use_global_device_ids=true, to_apply=%region_31.32 | all-reduce | flops 1 | bytes 8 | tf_op jit(solution)/shard_map/psum | solution.py:73
  549.1 32.0 %psum.156 = f32[]{:T(128)} all-reduce(f32[]{:T(128)} %get-tuple-element.55), channel_id=1, replica_groups=mesh['ens'=2,'lat'=16] {'lat'}, use_global_device_ids=true, to_apply=%region_33.34 | all-reduce | flops 1 | bytes 8 | tf_op jit(solution)/shard_map/psum | solution.py:61
  584.5 2.6 collective-permute-start.18
  590.3 28.1 %psum.157 = f32[]{:T(128)} all-reduce(f32[]{:T(128)} %get-tuple-element.53), channel_id=1, replica_groups=mesh['ens'=2,'lat'=16] {'lat'}, use_global_device_ids=true, to_apply=%region_35.36 | all-reduce | flops 1 | bytes 8 | tf_op jit(solution)/shard_map/psum | solution.py:73
  622.1 31.9 %psum.158 = f32[]{:T(128)} all-reduce(f32[]{:T(128)} %multiply_reduce_fusion), channel_id=1, replica_groups=mesh['ens'=2,'lat'=16] {'lat'}, use_global_device_ids=true, to_apply=%region_37.38 | all-reduce | flops 1 | bytes 8 | tf_op jit(solution)/shard_map/psum | solution.py:61
  657.4 2.6 collective-permute-start.20
  660.0 2.4 collective-permute-done.20
  664.8 28.2 %psum.159 = f32[]{:T(128)} all-reduce(f32[]{:T(128)} %fusion.77), channel_id=1, replica_groups=mesh['ens'=2,'lat'=16] {'lat'}, use_global_device_ids=true, to_apply=%region_39.40 | all-reduce | flops 1 | bytes 8 | tf_op jit(solution)/shard_map/psum | solution.py:73
  701.1 7.9 %stack.11 = f32[3,10,4,4320]{3,1,2,0:T(8,128)} concatenate(f32[3,1,4,4320]{3,1,2,0:T(1,128)S(1)} %get-tuple-element.22, f32[3,1,4,4320]{3,1,2,0:T(1,128)S(1)} %get-tuple-element.23, f32[3,1,4,4320]{3,1,2,0:T(1,128)S(1)} %get-tuple-element.24, f32[3,1,4,4320]{3,1,2,0:T(1,128)S(1)} %get-tuple-element.25, f32[3,1,4,4320]{3,1,2,0:T(1,128)S(1)} %get-tuple-element.26, ...), dimensions={1} | concatenate | bytes 4147200 | tf_op jit(solution)/shard_map/stack | solution.py:45
  709.0 2.7 broadcast_multiply_fusion
  711.7 4.0 broadcast_multiply_fusion.1
  716.7 4.5 collective-permute-start.22
  725.0 3.0 reverse.1
  729.6 4.8 slice.704
  740.9 17.1 %reverse = f32[3,10,1,4352]{3,1,2,0:T(8,128)} reverse(f32[3,10,1,4352]{3,1,2,0:T(8,128)} %bitcast.146), dimensions={3} | reverse | bytes 1044480
  758.0 5.9 fusion.1
  764.4 2.7 copy.12
  (199 shorter events, 73.5 us)
Async XLA Ops:
  0.6 13.9 %copy-start.7 = (s32[4,4320]{1,0:T(4,128)S(1)}, s32[4,4320]{1,0:T(4,128)}, u32[]{:S(2)}) copy-start(s32[4,4320]{1,0:T(4,128)} %param.18) | copy-start | bytes 207364
  0.6 13.9 %copy-start.6 = (f32[4,4320]{1,0:T(4,128)S(1)}, f32[4,4320]{1,0:T(4,128)}, u32[]{:S(2)}) copy-start(f32[4,4320]{1,0:T(4,128)} %param.16) | copy-start | bytes 207364
  0.7 14.2 %copy-start.8 = (f32[4,4320]{1,0:T(4,128)S(1)}, f32[4,4320]{1,0:T(4,128)}, u32[]{:S(2)}) copy-start(f32[4,4320]{1,0:T(4,128)} %param.12) | copy-start | bytes 207364
  0.7 14.2 %copy-start.40 = (f32[4,4320]{1,0:T(4,128)S(1)}, f32[4,4320]{1,0:T(4,128)}, u32[]{:S(2)}) copy-start(f32[4,4320]{1,0:T(4,128)} %param.17) | copy-start | bytes 207364
  2.7 12.0 %collective-permute-start = (f32[2,1,4320]{2,1,0:T(1,128)S(1)}, f32[2,1,4320]{2,1,0:T(1,128)S(1)}, u32[]{:S(2)}, u32[]{:S(2)}) collective-permute-start(f32[2,1,4320]{2,1,0:T(1,128)S(1)} %get-tuple-element.133), channel_id=1, source_target_pairs={{0,1},{1,2},{2,3},{3,4},{4,5},{5,6},{6,7},{7,8},{8,9},{9,10},{10,1... | collective-permute-start | bytes 103688 | tf_op jit(solution)/shard_map/ppermute | solution.py:16
  6.4 8.3 %collective-permute-start.1 = (f32[2,1,4320]{2,1,0:T(1,128)S(1)}, f32[2,1,4320]{2,1,0:T(1,128)S(1)}, u32[]{:S(2)}, u32[]{:S(2)}) collective-permute-start(f32[2,1,4320]{2,1,0:T(1,128)S(1)} %get-tuple-element.134), channel_id=1, source_target_pairs={{1,0},{2,1},{3,2},{4,3},{5,4},{6,5},{7,6},{8,7},{9,8},{10,9},{11,1... | collective-permute-start | bytes 103688 | tf_op jit(solution)/shard_map/ppermute | solution.py:17
  15.1 5.7 collective-permute-start.3
  18.8 5.1 collective-permute-start.2
  80.9 4.6 collective-permute-start.5
  82.8 5.1 collective-permute-start.4
  152.2 4.6 collective-permute-start.7
  154.2 5.1 collective-permute-start.6
  223.6 4.6 collective-permute-start.9
  225.5 5.1 collective-permute-start.8
  294.9 4.6 collective-permute-start.11
  296.8 5.1 collective-permute-start.10
  366.2 4.6 collective-permute-start.13
  368.1 5.1 collective-permute-start.12
  437.5 4.6 collective-permute-start.15
  439.5 5.1 collective-permute-start.14
  474.7 220.5 %copy-start.5 = (f32[3,10,4,4320]{3,2,1,0:T(4,128)S(1)}, f32[3,10,4,4320]{3,2,1,0:T(4,128)}, u32[]{:S(2)}) copy-start(f32[3,10,4,4320]{3,2,1,0:T(4,128)} %param.11) | copy-start | bytes 6220804
  509.5 4.6 collective-permute-start.17
  511.5 5.1 collective-permute-start.16
  582.6 4.6 collective-permute-start.19
  584.5 5.1 collective-permute-start.18
  655.4 4.6 collective-permute-start.21
  657.4 5.1 collective-permute-start.20
  664.8 31.7 %copy-start.18 = (f32[4,4320]{1,0:T(4,128)S(1)}, f32[4,4320]{1,0:T(4,128)}, u32[]{:S(2)}) copy-start(f32[4,4320]{1,0:T(4,128)} %get-tuple-element.100) | copy-start | bytes 207364
  664.8 31.7 %copy-start.19 = (f32[4,4320]{1,0:T(4,128)S(1)}, f32[4,4320]{1,0:T(4,128)}, u32[]{:S(2)}) copy-start(f32[4,4320]{1,0:T(4,128)} %get-tuple-element.101) | copy-start | bytes 207364
  664.8 31.7 %copy-start.20 = (f32[4,4320]{1,0:T(4,128)S(1)}, f32[4,4320]{1,0:T(4,128)}, u32[]{:S(2)}) copy-start(f32[4,4320]{1,0:T(4,128)} %get-tuple-element.102) | copy-start | bytes 207364
  696.4 2.6 copy-start.10
  696.5 2.6 copy-start.12
  696.5 2.6 copy-start.13
  696.5 2.6 copy-start.14
  696.5 2.6 copy-start.15
  701.1 7.9 %copy-start.38 = (f32[4,4320]{1,0:T(4,128)S(1)}, f32[4,4320]{1,0:T(4,128)}, u32[]{:S(2)}) copy-start(f32[4,4320]{1,0:T(4,128)} %get-tuple-element.130) | copy-start | bytes 207364
  709.0 2.7 copy-start.35
  709.0 2.7 copy-start.36
  709.0 2.7 copy-start.37
  711.7 9.5 %copy-start = (f32[3,10,4,4320]{3,1,2,0:T(8,128)}, f32[3,10,4,4320]{3,1,2,0:T(8,128)S(1)}, u32[]{:S(2)}) copy-start(f32[3,10,4,4320]{3,1,2,0:T(8,128)S(1)} %get-tuple-element.20) | copy-start | bytes 6220804
  715.7 6.4 copy-start.2
  715.7 13.0 %copy-start.41 = (s32[3,10]{1,0:T(4,128)S(1)}, s32[3,10]{1,0:T(4,128)}, u32[]{:S(2)}) copy-start(s32[3,10]{1,0:T(4,128)} %param.19) | copy-start | bytes 364
  716.7 41.2 %collective-permute-start.22 = (f32[3,10,1,4320]{3,1,2,0:T(8,128)}, f32[3,10,1,4320]{3,1,2,0:T(8,128)}, u32[]{:S(2)}, u32[]{:S(2)}) collective-permute-start(f32[3,10,1,4320]{3,1,2,0:T(8,128)} %slice.709), channel_id=1, source_target_pairs={{1,0},{2,1},{3,2},{4,3},{5,4},{6,5},{7,6},{8,7},{9,8},{10,9},{11,1... | collective-permute-start | bytes 1555208 | tf_op jit(solution)/shard_map/ppermute | solution.py:25
  722.1 35.8 %collective-permute-start.23 = (f32[3,10,1,4320]{3,1,2,0:T(8,128)}, f32[3,10,1,4320]{3,1,2,0:T(8,128)}, u32[]{:S(2)}, u32[]{:S(2)}) collective-permute-start(f32[3,10,1,4320]{3,1,2,0:T(8,128)} %slice.710), channel_id=1, source_target_pairs={{0,1},{1,2},{2,3},{3,4},{4,5},{5,6},{6,7},{7,8},{8,9},{9,10},{10,1... | collective-permute-start | bytes 1555208 | tf_op jit(solution)/shard_map/ppermute | solution.py:25
  729.6 4.8 copy-start.3
  734.3 2.9 copy-start.1
  758.0 5.9 copy-start.4
  758.0 5.9 copy-start.39
  (18 other events, 41.1 us)
where the time goes:
time: 781 us; the launch traced here: 767 us
  blocking collectives  561 us (72%)
  starting transfers between devices  57.8 us (7%)
  local copies, waits for them, and re-layouts  52 us (7%)
  other arithmetic  43.9 us (6%)
  between operations  26.9 us (3%)
  waiting for transfers between devices  25 us (3%)
    psum x10, blocking collectives, residual_norm(): return lax.psum(jnp.sum(residual * scaled), 'lat')  309 us
    psum x9, blocking collectives, classic_solve(): step_size = norm_now / lax.psum(jnp.sum(direction * applied), 'lat')  253 us
    ppermute x11, starting transfers between devices, padded(): after = lax.ppermute(initial, axis, down)  26.8 us
    ppermute x11, waiting for transfers between devices, padded(): after = lax.ppermute(initial, axis, down)  24.9 us
    ppermute x11, starting transfers between devices, padded(): before = lax.ppermute(last, axis, up)  24.6 us
    unnamed x87, local copies, waits for them, and re-layouts  24.1 us
  transfers between devices with their start and end apart: 24, of which 10 were waited for; matrix products, arithmetic and copies ran while one was open for 5% of the time, Pallas kernels for 0%

commit v1 on v0

v1 whole, which is shorter than its diff:
```python
import functools

import jax
import jax.numpy as jnp
from jax import lax
from jax.experimental import pallas as pl
from jax.experimental.pallas import tpu as pltpu
from jax.sharding import PartitionSpec as P

ITERS = 10
LANES = 128
ROWS = 8
MESH = pl.DeviceIdType.MESH


def kernel(
    count, block, nx, variables, levels,
    cot_ref, surf_in, stencil_ref, mix_ref, weights_ref, depth_ref, mass_ref, ocean_ref, fold_ref,
    out_ref, surface_ref,
    gathered, pbuf, qbuf, rbuf, ebuf, nbuf, sbuf, xbuf, surface_ext, dbuf, wbuf,
    cot_ext, mix_ext, coef_ext, flipped, reverse_in,
    up_out, down_out, up_in, down_in,
    zs, zr, ys, yr, cs, cr, hs, hr,
):
    tiles = -(-nx // LANES)
    tail = nx - (tiles - 1) * LANES
    width = tiles * LANES
    depths = count // 4
    total_rows = count * block
    row_tiles = total_rows // ROWS
    fields = variables * levels

    me = lax.axis_index("lat")
    core = me % 2
    side = (me // 2) % 2
    plane = me // 4

    def index_of(z, y, c):
        return (z * 2 + y) * 2 + c

    def span(c):
        return slice(c * LANES, min(nx, (c + 1) * LANES))

    def cols(c):
        return slice(c * LANES, (c + 1) * LANES)

    def copy(src, dst, ssem, rsem, to):
        return pltpu.make_async_remote_copy(
            src_ref=src, dst_ref=dst, send_sem=ssem, recv_sem=rsem, device_id={"lat": to}, device_id_type=MESH
        )

    other_side = index_of(plane, 1 - side, core)
    other_core = index_of(plane, side, 1 - core)
    above = (me + 1) % count
    below = (me + count - 1) % count
    planes = [(plane + d) % depths for d in range(1, depths)]

    barrier = pltpu.get_barrier_semaphore()
    partners = [index_of(z, side, core) for z in planes] + [other_side, other_core, above, below]
    for partner in partners:
        pl.semaphore_signal(barrier, inc=1, device_id={"lat": partner}, device_id_type=MESH)

    wet_own = ocean_ref[...].astype(jnp.float32)
    gathered[me, 0] = depth_ref[...]
    gathered[me, 1] = wet_own
    gathered[me, 2] = mass_ref[...]
    gathered[me, 3] = wet_own * surf_in[...]
    pl.semaphore_wait(barrier, len(partners))

    sent = []

    def send(src_index, ssem, rsem, to):
        c = copy(gathered.at[src_index], gathered.at[src_index], ssem, rsem, to)
        c.start()
        sent.append(c)

    def arrived(src_index, ssem, rsem):
        copy(gathered.at[src_index], gathered.at[src_index], ssem, rsem, other_core).wait_recv()

    for z in planes:
        send(me, zs.at[z], zr.at[plane], index_of(z, side, core))
    send(me, ys.at[plane], yr.at[plane], other_side)
    send(me, cs.at[plane], cr.at[plane], other_core)

    for v in range(variables):
        for k in range(levels):
            up_out[pl.ds(v * levels + k, 1)] = cot_ref[v, k, block - 1:block, :]
            down_out[pl.ds(v * levels + k, 1)] = cot_ref[v, k, 0:1, :]
    for k in range(levels - 1):
        up_out[pl.ds(fields + k, 1)] = mix_ref[k, block - 1:block, :]
        down_out[pl.ds(fields + k, 1)] = mix_ref[k, 0:1, :]
    up_out[pl.ds(fields + levels - 1, 1)] = stencil_ref[4, block - 1:block, :]
    down_out[pl.ds(fields + levels - 1, 1)] = stencil_ref[3, 0:1, :]

    for z in planes:
        source = index_of(z, side, core)
        arrived(source, zs.at[z], zr.at[z])
        send(source, ys.at[z], yr.at[z], other_side)
        send(source, cs.at[z], cr.at[z], other_core)

    def ext_zero(ref):
        ref[:, :, (tiles - 1) * LANES:] = jnp.zeros(ref.shape[:2] + (LANES,), jnp.float32)
        ref[:, block:, :] = jnp.zeros((ref.shape[0], ROWS - block, width), jnp.float32)

    for ref in (cot_ext, mix_ext, coef_ext):
        ext_zero(ref)
    reverse_in[...] = jnp.zeros_like(reverse_in)
    damped = cot_ext
    for v in range(variables):
        cot_ext[pl.ds(v * levels, levels), 0:block, 0:nx] = cot_ref[v]
    mix_ext[:, 0:block, 0:nx] = mix_ref[...]
    coef_ext[:, 0:block, 0:nx] = stencil_ref[...]
    for ref in (pbuf, qbuf, rbuf):
        ref[:, :, (tiles - 1) * LANES:] = jnp.zeros((row_tiles + 2, ROWS, LANES), jnp.float32)
    xbuf[...] = jnp.zeros_like(xbuf)

    for z in [plane] + planes:
        source = index_of(z, 1 - side, core)
        arrived(source, ys.at[z], yr.at[z])
        send(source, cs.at[depths + z], cr.at[depths + z], other_core)

    halo_up = copy(up_out, up_in, hs.at[0], hr.at[0], above)
    halo_down = copy(down_out, down_in, hs.at[1], hr.at[1], below)
    halo_up.start()
    halo_down.start()

    for z in [plane] + planes:
        arrived(index_of(z, side, 1 - core), cs.at[z], cr.at[z])
        arrived(index_of(z, 1 - side, 1 - core), cs.at[depths + z], cr.at[depths + z])

    lane = lax.broadcasted_iota(jnp.int32, (ROWS, LANES), 1)
    sub = lax.broadcasted_iota(jnp.int32, (ROWS, LANES), 0)

    def roll(x, by):
        return pltpu.roll(x, by % LANES, 1)

    def east(get):
        first = get(0)
        now = first
        for c in range(tiles):
            if c < tiles - 1:
                after = get(c + 1)
                yield c, jnp.where(lane == LANES - 1, roll(after, -1), roll(now, -1))
                now = after
            else:
                yield c, jnp.where(lane == tail - 1, roll(first, tail - 1), roll(now, -1))

    def west(get):
        before = roll(get(tiles - 1), LANES - tail + 1)
        for c in range(tiles):
            x = get(c)
            if c == tiles - 1:
                x = jnp.where(lane < tail - 1, x, 0.0)
            rolled = roll(x, 1)
            yield c, jnp.where(lane == 0, before, rolled)
            before = rolled

    def wrap(ref):
        ref[0] = pltpu.roll(ref[row_tiles], 1, 0)
        ref[row_tiles + 1] = pltpu.roll(ref[1], ROWS - 1, 0)

    strip = row_tiles // block

    def place(t, carry, targets):
        for r in range(block):
            for field, ref in targets:
                for c in range(tiles):
                    parts = [gathered[s * strip + t, field, r:r + 1, span(c)] for s in range(ROWS)]
                    ref[t * block + r + 1, :, span(c)] = jnp.concatenate(parts, axis=0)
        return carry

    lax.fori_loop(0, strip, functools.partial(place, targets=((0, pbuf), (1, qbuf), (2, rbuf))), 0)
    wrap(pbuf)
    wrap(qbuf)

    for field, ref in ((0, dbuf), (1, wbuf)):
        ref[...] = jnp.zeros_like(ref)
        ref[0:block, 0:nx] = gathered[me, field]
        ref[block:block + 1, 0:nx] = gathered[above, field, 0:1]
        ref[ROWS - 1:ROWS, 0:nx] = gathered[below, field, block - 1:block]

    def links(t, carry):
        for (c, de), (_, we) in zip(east(lambda c: pbuf[t, :, cols(c)]), east(lambda c: qbuf[t, :, cols(c)])):
            d, w = pbuf[t, :, cols(c)], qbuf[t, :, cols(c)]
            ebuf[t, :, cols(c)] = 0.5 * (d + de) * w * we
            nbuf[t, :, cols(c)] = 0.5 * (d + pbuf[t + 1, :, cols(c)]) * w * qbuf[t + 1, :, cols(c)]
        return carry

    lax.fori_loop(1, row_tiles + 1, links, 0)
    for c in range(tiles):
        nbuf[row_tiles, :, cols(c)] = jnp.where(sub == ROWS - 1, 0.0, nbuf[row_tiles, :, cols(c)])
    wrap(nbuf)

    def scales(t, carry):
        for c, ew in west(lambda c: ebuf[t, :, cols(c)]):
            centre = rbuf[t, :, cols(c)] + ebuf[t, :, cols(c)] + ew + nbuf[t, :, cols(c)] + nbuf[t - 1, :, cols(c)]
            if c == tiles - 1:
                centre = jnp.where(lane < tail, centre, 1.0)
            qbuf[t, :, cols(c)] = 1.0 / jnp.sqrt(centre)
        return carry

    lax.fori_loop(1, row_tiles + 1, scales, 0)
    wrap(qbuf)
    lax.fori_loop(0, strip, functools.partial(place, targets=((3, rbuf),)), 0)

    def rescale(t, carry):
        for c, se in east(lambda c: qbuf[t, :, cols(c)]):
            s = qbuf[t, :, cols(c)]
            ebuf[t, :, cols(c)] = ebuf[t, :, cols(c)] * s * se
            nbuf[t, :, cols(c)] = nbuf[t, :, cols(c)] * s * qbuf[t + 1, :, cols(c)]
        return carry

    lax.fori_loop(1, row_tiles + 1, rescale, 0)
    wrap(nbuf)

    zero = jnp.zeros((ROWS, LANES), jnp.float32)

    def begin(t, acc):
        for c in range(tiles):
            r = rbuf[t, :, cols(c)] * qbuf[t, :, cols(c)]
            rbuf[t, :, cols(c)] = r
            pbuf[t, :, cols(c)] = r
            acc = acc + r * r
        return acc

    norm = jnp.sum(lax.fori_loop(1, row_tiles + 1, begin, zero))
    wrap(pbuf)
    own_tile = (me % strip) * block
    for m in range(block + 2):
        sbuf[m] = qbuf[own_tile + m]

    def iterate(_, norm):
        def apply(t, acc):
            acc = list(acc)
            for (c, pe), (_, pw) in zip(
                east(lambda c: pbuf[t, :, cols(c)]), west(lambda c: ebuf[t, :, cols(c)] * pbuf[t, :, cols(c)])
            ):
                p = pbuf[t, :, cols(c)]
                q = (p - ebuf[t, :, cols(c)] * pe - pw) - (
                    nbuf[t, :, cols(c)] * pbuf[t + 1, :, cols(c)] + nbuf[t - 1, :, cols(c)] * pbuf[t - 1, :, cols(c)]
                )
                qbuf[t, :, cols(c)] = q
                acc[c % 2] = acc[c % 2] + p * q
            return tuple(acc)

        a, b = lax.fori_loop(1, row_tiles + 1, apply, (zero, zero))
        step = norm / jnp.sum(a + b)

        def advance(m, carry):
            for c in range(tiles):
                xbuf[m, :, cols(c)] = xbuf[m, :, cols(c)] + step * pbuf[own_tile + m, :, cols(c)]
            return carry

        lax.fori_loop(0, block + 2, advance, 0)

        def residual(t, acc):
            acc = list(acc)
            for c in range(tiles):
                r = rbuf[t, :, cols(c)] - step * qbuf[t, :, cols(c)]
                rbuf[t, :, cols(c)] = r
                acc[c % 2] = acc[c % 2] + r * r
            return tuple(acc)

        a, b = lax.fori_loop(1, row_tiles + 1, residual, (zero, zero))
        new = jnp.sum(a + b)
        ratio = new / norm

        def direct(t, carry):
            for c in range(tiles):
                pbuf[t, :, cols(c)] = rbuf[t, :, cols(c)] + ratio * pbuf[t, :, cols(c)]
            return carry

        lax.fori_loop(1, row_tiles + 1, direct, 0)
        wrap(pbuf)
        return new

    lax.fori_loop(0, ITERS, iterate, norm)

    mine = jnp.where(sub == me // strip, 1.0, 0.0)
    surface_ext[...] = jnp.zeros_like(surface_ext)
    for c in range(tiles):
        for m, row in enumerate([ROWS - 1] + list(range(block + 1))):
            x = xbuf[m, :, cols(c)] * sbuf[m, :, cols(c)] * mine
            surface_ext[row:row + 1, cols(c)] = jnp.sum(x, axis=0, keepdims=True)
    surface_ref[...] = surface_ext[0:block, 0:nx]
    dbuf[...] = dbuf[...] * surface_ext[...]

    halo_up.wait()
    halo_down.wait()
    has_above = jnp.where(me < count - 1, 1.0, 0.0)
    has_below = jnp.where(me > 0, 1.0, 0.0)
    for f in range(fields):
        cot_ext[f, block:block + 1, 0:nx] = down_in[pl.ds(f, 1)]
        cot_ext[f, ROWS - 1:ROWS, 0:nx] = up_in[pl.ds(f, 1)]
    for k in range(levels - 1):
        mix_ext[k, block:block + 1, 0:nx] = down_in[pl.ds(fields + k, 1)]
        mix_ext[k, ROWS - 1:ROWS, 0:nx] = up_in[pl.ds(fields + k, 1)]
    coef_ext[3, block:block + 1, 0:nx] = down_in[pl.ds(fields + levels - 1, 1)] * has_above
    coef_ext[4, ROWS - 1:ROWS, 0:nx] = up_in[pl.ds(fields + levels - 1, 1)] * has_below

    def solve(c, carry):
        at = pl.ds(pl.multiple_of(c * LANES, LANES), LANES)
        mixes = [mix_ext[k, :, at] for k in range(levels - 1)]
        ratios, inverses = [], []
        for k in range(levels):
            under = mixes[k - 1] if k > 0 else 0.0
            over = mixes[k] if k < levels - 1 else 0.0
            pivot = 1.0 + under + over
            if k > 0:
                pivot = pivot + under * ratios[-1]
            inverse = 1.0 / pivot
            inverses.append(inverse)
            ratios.append(-over * inverse)
        lift, wet, north = dbuf[:, at], wbuf[:, at], coef_ext[4, :, at]
        for v in range(variables):
            reduced = []
            for k in range(levels):
                source = cot_ext[v * levels + k, :, at] + weights_ref[v, k] * lift
                if k > 0:
                    source = source + mixes[k - 1] * reduced[-1]
                reduced.append(source * inverses[k])
            result = reduced[-1]
            for k in range(levels - 1, -1, -1):
                if k < levels - 1:
                    result = reduced[k] - ratios[k] * result
                value = wet * result
                damped[v * levels + k, :, at] = value
                reverse_in[pl.ds(v * levels + k, 1), at] = (north * value)[block - 1:block]
        return carry

    lax.fori_loop(0, tiles, solve, 0)

    flag = jnp.where(me == count - 1, 1.0, 0.0)
    height = reverse_in.shape[0]
    a = lax.broadcasted_iota(jnp.int32, (2 * LANES, LANES), 0)
    b = lax.broadcasted_iota(jnp.int32, (2 * LANES, LANES), 1)
    permute = jnp.where(a + b == LANES + tail - 1, 1.0, 0.0)
    for c in range(tiles):
        if c < tiles - 1:
            x, m = reverse_in[:, (tiles - 2 - c) * LANES:(tiles - c) * LANES], permute
        else:
            x, m = reverse_in[:, 0:LANES], permute[LANES:]
        turned = jnp.dot(x, m, precision=lax.Precision.HIGHEST, preferred_element_type=jnp.float32)
        flipped[:, :, cols(c)] = turned[:, None, :]

    def horizontal(f, carry):
        sign = (2 * fold_ref[f // levels, f % levels] - 1).astype(jnp.float32) * flag
        for (c, pe), (_, pw) in zip(
            east(lambda c: coef_ext[1, :, cols(c)] * damped[f, :, cols(c)]),
            west(lambda c: coef_ext[2, :, cols(c)] * damped[f, :, cols(c)]),
        ):
            d = damped[f, :, cols(c)]
            value = (
                coef_ext[0, :, cols(c)] * d + pe + pw
                + pltpu.roll(coef_ext[3, :, cols(c)] * d, ROWS - 1, 0)
                + pltpu.roll(coef_ext[4, :, cols(c)] * d, 1, 0)
            )
            value = value + jnp.where(sub == block - 1, sign * flipped[f, :, cols(c)], 0.0)
            out_ref[f // levels, f % levels, :, span(c)] = value[0:block, 0:span(c).stop - span(c).start]
        return carry

    lax.fori_loop(0, fields, horizontal, 0)

    for c in sent:
        c.wait_send()


def solution(mesh):
    count = mesh.shape["lat"]
    in_specs = (
        P("ens", None, "lat", None),
        P(("ens", "lat"), None),
        P(None, "lat", None),
        P(None, "lat", None),
        P(),
        P("lat", None),
        P("lat", None),
        P("lat", None),
        P(),
    )
    out_specs = (P("ens", None, "lat", None), P(("ens", "lat"), None))

    def shards(cot_next, cot_surface, stencil, mix, weights, depth, surface_mass, ocean, fold_sign):
        variables, levels, block, nx = cot_next.shape
        width = -(-nx // LANES) * LANES
        row_tiles = count * block // ROWS
        depths = count // 4
        fields = variables * levels
        vmem = pl.BlockSpec(memory_space=pltpu.VMEM)
        smem = pl.BlockSpec(memory_space=pltpu.SMEM)
        f32 = jnp.float32
        ext = pltpu.VMEM((ROWS, width), f32)
        dma = pltpu.SemaphoreType.DMA
        return pl.pallas_call(
            functools.partial(kernel, count, block, nx, variables, levels),
            out_shape=(jax.ShapeDtypeStruct(cot_next.shape, f32), jax.ShapeDtypeStruct(cot_surface.shape, f32)),
            in_specs=[vmem, vmem, vmem, vmem, smem, vmem, vmem, vmem, smem],
            out_specs=(vmem, vmem),
            scratch_shapes=[
                pltpu.VMEM((count, 4, block, nx), f32),
                *[pltpu.VMEM((row_tiles + 2, ROWS, width), f32) for _ in range(5)],
                pltpu.VMEM((block + 2, ROWS, width), f32),
                pltpu.VMEM((block + 2, ROWS, width), f32),
                ext, ext, ext,
                pltpu.VMEM((fields, ROWS, width), f32),
                pltpu.VMEM((levels - 1, ROWS, width), f32),
                pltpu.VMEM((5, ROWS, width), f32),
                pltpu.VMEM((-(-fields // 8) * 8, 1, width), f32),
                pltpu.VMEM((-(-fields // 8) * 8, width), f32),
                *[pltpu.VMEM((fields + levels, nx), f32) for _ in range(4)],
                dma((depths,)), dma((depths,)), dma((depths,)), dma((depths,)),
                dma((2 * depths,)), dma((2 * depths,)), dma((2,)), dma((2,)),
            ],
            compiler_params=pltpu.CompilerParams(
                collective_id=0, has_side_effects=True, vmem_limit_bytes=60 * 1024 * 1024
            ),
        )(cot_next, cot_surface, stencil, mix, weights, depth, surface_mass, ocean, fold_sign)

    return jax.shard_map(shards, mesh=mesh, in_specs=in_specs, out_specs=out_specs, check_vma=False)
```

time: 781 us -> 104 us (0.13); the launches traced: 767 us -> 104 us
  blocking collectives: 561 us -> 0 us
  Pallas kernels: 0 us -> 99.9 us
  starting transfers between devices: 57.8 us -> 0 us
  local copies, waits for them, and re-layouts: 52 us -> 3.7 us
  other arithmetic: 43.9 us -> 0 us
  between operations: 26.9 us -> 0.65 us
  waiting for transfers between devices: 25 us -> 0 us
    psum x19 -> x0, blocking collectives: 561 us -> none  [the longest x10 309 us: residual_norm(): return lax.psum(jnp.sum(residual * scaled), 'lat')]
    pallas_call x0 -> x1, Pallas kernels: none -> 99.9 us  [shards(): pl.pallas_call(functools.partial(kernel, count, block, nx, variables, lev...]
    ppermute x24 -> x0, starting transfers between devices: 57.8 us -> none  [the longest x11 26.8 us: padded(): after = lax.ppermute(initial, axis, down)]
    ppermute x24 -> x0, waiting for transfers between devices: 25 us -> none  [the longest x11 24.9 us: padded(): after = lax.ppermute(initial, axis, down)]
    unnamed x87 -> x4, local copies, waits for them, and re-layouts: 24.1 us -> 3.7 us
    slice x44 -> x0, local copies, waits for them, and re-layouts: 17.6 us -> none  [the longest x2 5.65 us: shards(): jnp.roll(west_c * damped, -1, -1)]
    reduce_sum x19 -> x0, other arithmetic: 15.9 us -> none  [the longest x10 8.43 us: classic_solve(): step_size = norm_now / lax.psum(jnp.sum(direction * applied), 'lat')]
    mul x6 -> x0, other arithmetic: 9.88 us -> none  [the longest x1 3.98 us: shards(): lifted = south_c * damped]
  transfers between devices with their start and end apart: 24 -> 0, of which waited for: 10 -> 0; matrix products, arithmetic and copies ran while one was open for 5% -> 0% of each run, Pallas kernels for 0% -> 0%
where the time goes in v1:
time: 104 us
  Pallas kernels  99.9 us (96%)
  local copies, waits for them, and re-layouts  3.7 us (4%)
    pallas_call x1, Pallas kernels, shards(): pl.pallas_call(functools.partial(kernel, count, block, nx, variables, lev...  99.9 us
    unnamed x4, local copies, waits for them, and re-layouts  3.7 us

profile of v1, /device:TPU:11, one launch (start us, length us, event | category | flops | bytes accessed | tf_op | source)
XLA Modules:
  0.0 104.2 jit_solution(11799073473829566833)
XLA Ops:
  0.6 99.9 %shard_map.104 = (f32[3,10,4,4320]{3,2,1,0:T(4,128)}, f32[4,4320]{1,0:T(4,128)}) custom-call(f32[3,10,4,4320]{3,2,1,0:T(4,128)} %cot_ref.1, f32[4,4320]{1,0:T(4,128)} %surf_in.1, f32[5,4,4320]{2,1,0:T(4,128)} %stencil_ref.1, f32[9,4,4320]{2,1,0:T(4,128)} %mix_ref.1, f32[3,10]{1,0:T(4,128)} %weights_ref.1, f32[4,4320]{1,0:T(4,128)} %depth_ref.1, ...), custom_call_target="tpu_custom_call" | custom-call | tf_op jit(solution)/shard_map/pallas_call | solution.py:394
  100.5 0.0 copy-start
  100.5 3.1 %copy.13 = f32[3,10,4,4320]{3,2,1,0:T(4,128)} copy(f32[3,10,4,4320]{3,2,1,0:T(4,128)} %get-tuple-element.4) | data formatting | bytes 4147200
  103.6 0.0 copy-done
  103.6 0.6 copy.14
Async XLA Ops:
  100.5 3.1 %copy-start = (f32[4,4320]{1,0:T(4,128)S(1)}, f32[4,4320]{1,0:T(4,128)}, u32[]{:S(2)}) copy-start(f32[4,4320]{1,0:T(4,128)} %get-tuple-element.5) | copy-start | bytes 207364

commit v2 on v1

--- a/solution.py
+++ b/solution.py
@@ -61,26 +61,29 @@
         pl.semaphore_signal(barrier, inc=1, device_id={"lat": partner}, device_id_type=MESH)
 
     wet_own = ocean_ref[...].astype(jnp.float32)
-    gathered[me, 0] = depth_ref[...]
-    gathered[me, 1] = wet_own
-    gathered[me, 2] = mass_ref[...]
-    gathered[me, 3] = wet_own * surf_in[...]
+    gathered[0, me] = depth_ref[...]
+    gathered[1, me] = wet_own
+    gathered[2, me] = mass_ref[...]
+    gathered[3, me] = wet_own * surf_in[...]
     pl.semaphore_wait(barrier, len(partners))
 
     sent = []
 
-    def send(src_index, ssem, rsem, to):
-        c = copy(gathered.at[src_index], gathered.at[src_index], ssem, rsem, to)
+    def send(field, src_index, ssem, rsem, to):
+        part = gathered.at[field, src_index]
+        c = copy(part, part, ssem, rsem, to)
         c.start()
         sent.append(c)
 
-    def arrived(src_index, ssem, rsem):
-        copy(gathered.at[src_index], gathered.at[src_index], ssem, rsem, other_core).wait_recv()
-
-    for z in planes:
-        send(me, zs.at[z], zr.at[plane], index_of(z, side, core))
-    send(me, ys.at[plane], yr.at[plane], other_side)
-    send(me, cs.at[plane], cr.at[plane], other_core)
+    def arrived(field, src_index, ssem, rsem):
+        part = gathered.at[field, src_index]
+        copy(part, part, ssem, rsem, other_core).wait_recv()
+
+    for f in range(4):
+        for z in planes:
+            send(f, me, zs.at[f, z], zr.at[f, plane], index_of(z, side, core))
+        send(f, me, ys.at[f, plane], yr.at[f, plane], other_side)
+        send(f, me, cs.at[f, plane], cr.at[f, plane], other_core)
 
     for v in range(variables):
         for k in range(levels):
@@ -91,12 +94,6 @@
         down_out[pl.ds(fields + k, 1)] = mix_ref[k, 0:1, :]
     up_out[pl.ds(fields + levels - 1, 1)] = stencil_ref[4, block - 1:block, :]
     down_out[pl.ds(fields + levels - 1, 1)] = stencil_ref[3, 0:1, :]
-
-    for z in planes:
-        source = index_of(z, side, core)
-        arrived(source, zs.at[z], zr.at[z])
-        send(source, ys.at[z], yr.at[z], other_side)
-        send(source, cs.at[z], cr.at[z], other_core)
 
     def ext_zero(ref):
         ref[:, :, (tiles - 1) * LANES:] = jnp.zeros(ref.shape[:2] + (LANES,), jnp.float32)
@@ -114,19 +111,34 @@
         ref[:, :, (tiles - 1) * LANES:] = jnp.zeros((row_tiles + 2, ROWS, LANES), jnp.float32)
     xbuf[...] = jnp.zeros_like(xbuf)
 
-    for z in [plane] + planes:
-        source = index_of(z, 1 - side, core)
-        arrived(source, ys.at[z], yr.at[z])
-        send(source, cs.at[depths + z], cr.at[depths + z], other_core)
+    def from_planes(f):
+        for z in planes:
+            source = index_of(z, side, core)
+            arrived(f, source, zs.at[f, z], zr.at[f, z])
+            send(f, source, ys.at[f, z], yr.at[f, z], other_side)
+            send(f, source, cs.at[f, z], cr.at[f, z], other_core)
+
+    def from_side(f):
+        for z in [plane] + planes:
+            source = index_of(z, 1 - side, core)
+            arrived(f, source, ys.at[f, z], yr.at[f, z])
+            send(f, source, cs.at[f, depths + z], cr.at[f, depths + z], other_core)
+
+    def from_core(f):
+        for z in [plane] + planes:
+            arrived(f, index_of(z, side, 1 - core), cs.at[f, z], cr.at[f, z])
+            arrived(f, index_of(z, 1 - side, 1 - core), cs.at[f, depths + z], cr.at[f, depths + z])
 
     halo_up = copy(up_out, up_in, hs.at[0], hr.at[0], above)
     halo_down = copy(down_out, down_in, hs.at[1], hr.at[1], below)
-    halo_up.start()
-    halo_down.start()
-
-    for z in [plane] + planes:
-        arrived(index_of(z, side, 1 - core), cs.at[z], cr.at[z])
-        arrived(index_of(z, 1 - side, 1 - core), cs.at[depths + z], cr.at[depths + z])
+
+    from_planes(0)
+    from_planes(1)
+    from_side(0)
+    from_planes(2)
+    from_side(1)
+    from_planes(3)
+    from_side(2)
 
     lane = lax.broadcasted_iota(jnp.int32, (ROWS, LANES), 1)
     sub = lax.broadcasted_iota(jnp.int32, (ROWS, LANES), 0)
@@ -165,19 +177,28 @@
         for r in range(block):
             for field, ref in targets:
                 for c in range(tiles):
-                    parts = [gathered[s * strip + t, field, r:r + 1, span(c)] for s in range(ROWS)]
+                    parts = [gathered[field, s * strip + t, r:r + 1, span(c)] for s in range(ROWS)]
                     ref[t * block + r + 1, :, span(c)] = jnp.concatenate(parts, axis=0)
         return carry
 
-    lax.fori_loop(0, strip, functools.partial(place, targets=((0, pbuf), (1, qbuf), (2, rbuf))), 0)
+    def place_all(field, ref):
+        lax.fori_loop(0, strip, functools.partial(place, targets=((field, ref),)), 0)
+
+    from_core(0)
+    place_all(0, pbuf)
+    from_core(1)
+    from_side(3)
+    halo_up.start()
+    halo_down.start()
+    place_all(1, qbuf)
     wrap(pbuf)
     wrap(qbuf)
 
     for field, ref in ((0, dbuf), (1, wbuf)):
         ref[...] = jnp.zeros_like(ref)
-        ref[0:block, 0:nx] = gathered[me, field]
-        ref[block:block + 1, 0:nx] = gathered[above, field, 0:1]
-        ref[ROWS - 1:ROWS, 0:nx] = gathered[below, field, block - 1:block]
+        ref[0:block, 0:nx] = gathered[field, me]
+        ref[block:block + 1, 0:nx] = gathered[field, above, 0:1]
+        ref[ROWS - 1:ROWS, 0:nx] = gathered[field, below, block - 1:block]
 
     def links(t, carry):
         for (c, de), (_, we) in zip(east(lambda c: pbuf[t, :, cols(c)]), east(lambda c: qbuf[t, :, cols(c)])):
@@ -190,6 +211,9 @@
     for c in range(tiles):
         nbuf[row_tiles, :, cols(c)] = jnp.where(sub == ROWS - 1, 0.0, nbuf[row_tiles, :, cols(c)])
     wrap(nbuf)
+
+    from_core(2)
+    place_all(2, rbuf)
 
     def scales(t, carry):
         for c, ew in west(lambda c: ebuf[t, :, cols(c)]):
@@ -201,7 +225,8 @@
 
     lax.fori_loop(1, row_tiles + 1, scales, 0)
     wrap(qbuf)
-    lax.fori_loop(0, strip, functools.partial(place, targets=((3, rbuf),)), 0)
+    from_core(3)
+    place_all(3, rbuf)
 
     def rescale(t, carry):
         for c, se in east(lambda c: qbuf[t, :, cols(c)]):
@@ -397,7 +422,7 @@
             in_specs=[vmem, vmem, vmem, vmem, smem, vmem, vmem, vmem, smem],
             out_specs=(vmem, vmem),
             scratch_shapes=[
-                pltpu.VMEM((count, 4, block, nx), f32),
+                pltpu.VMEM((4, count, block, nx), f32),
                 *[pltpu.VMEM((row_tiles + 2, ROWS, width), f32) for _ in range(5)],
                 pltpu.VMEM((block + 2, ROWS, width), f32),
                 pltpu.VMEM((block + 2, ROWS, width), f32),
@@ -408,8 +433,8 @@
                 pltpu.VMEM((-(-fields // 8) * 8, 1, width), f32),
                 pltpu.VMEM((-(-fields // 8) * 8, width), f32),
                 *[pltpu.VMEM((fields + levels, nx), f32) for _ in range(4)],
-                dma((depths,)), dma((depths,)), dma((depths,)), dma((depths,)),
-                dma((2 * depths,)), dma((2 * depths,)), dma((2,)), dma((2,)),
+                dma((4, depths)), dma((4, depths)), dma((4, depths)), dma((4, depths)),
+                dma((4, 2 * depths)), dma((4, 2 * depths)), dma((2,)), dma((2,)),
             ],
             compiler_params=pltpu.CompilerParams(
                 collective_id=0, has_side_effects=True, vmem_limit_bytes=60 * 1024 * 1024

time: 104 us -> 92.7 us (0.89)
  Pallas kernels: 99.9 us -> 87.9 us
    pallas_call x1, Pallas kernels: 99.9 us -> 87.9 us  [shards(): pl.pallas_call(functools.partial(kernel, count, block, nx, variables, lev...]
where the time goes in v2:
time: 92.7 us; the launch traced here: 92.2 us
  Pallas kernels  87.9 us (95%)
  local copies, waits for them, and re-layouts  3.7 us (4%)
    pallas_call x1, Pallas kernels, shards(): pl.pallas_call(functools.partial(kernel, count, block, nx, variables, lev...  87.9 us
    unnamed x4, local copies, waits for them, and re-layouts  3.7 us

profile of v2, /device:TPU:11, one launch (start us, length us, event | category | flops | bytes accessed | tf_op | source)
XLA Modules:
  0.0 92.2 jit_solution(15250520711559031991)
XLA Ops:
  0.6 87.9 %shard_map.104 = (f32[3,10,4,4320]{3,2,1,0:T(4,128)}, f32[4,4320]{1,0:T(4,128)}) custom-call(f32[3,10,4,4320]{3,2,1,0:T(4,128)} %cot_ref.1, f32[4,4320]{1,0:T(4,128)} %surf_in.1, f32[5,4,4320]{2,1,0:T(4,128)} %stencil_ref.1, f32[9,4,4320]{2,1,0:T(4,128)} %mix_ref.1, f32[3,10]{1,0:T(4,128)} %weights_ref.1, f32[4,4320]{1,0:T(4,128)} %depth_ref.1, ...), custom_call_target="tpu_custom_call" | custom-call | tf_op jit(solution)/shard_map/pallas_call | solution.py:419
  88.5 0.0 copy-start
  88.5 3.1 %copy.13 = f32[3,10,4,4320]{3,2,1,0:T(4,128)} copy(f32[3,10,4,4320]{3,2,1,0:T(4,128)} %get-tuple-element.4) | data formatting | bytes 4147200
  91.6 0.0 copy-done
  91.6 0.6 copy.14
Async XLA Ops:
  88.5 3.1 %copy-start = (f32[4,4320]{1,0:T(4,128)S(1)}, f32[4,4320]{1,0:T(4,128)}, u32[]{:S(2)}) copy-start(f32[4,4320]{1,0:T(4,128)} %get-tuple-element.5) | copy-start | bytes 207364

commit v3 on v2

--- a/solution.py
+++ b/solution.py
@@ -14,13 +14,13 @@
 
 
 def kernel(
-    count, block, nx, variables, levels,
+    members, count, block, nx, variables, levels,
     cot_ref, surf_in, stencil_ref, mix_ref, weights_ref, depth_ref, mass_ref, ocean_ref, fold_ref,
     out_ref, surface_ref,
-    gathered, pbuf, qbuf, rbuf, ebuf, nbuf, sbuf, xbuf, surface_ext, dbuf, wbuf,
+    shared, right, pbuf, qbuf, rbuf, ebuf, nbuf, sbuf, xbuf, surface_ext, dbuf, wbuf,
     cot_ext, mix_ext, coef_ext, flipped, reverse_in,
     up_out, down_out, up_in, down_in,
-    zs, zr, ys, yr, cs, cr, hs, hr,
+    zs, zr, ys, yr, cs, cr, os, orx, xs, xr, fs, fr, hs, hr,
 ):
     tiles = -(-nx // LANES)
     tail = nx - (tiles - 1) * LANES
@@ -30,7 +30,12 @@
     row_tiles = total_rows // ROWS
     fields = variables * levels
 
+    part_tiles = -(-tiles // members)
+    part_width = part_tiles * LANES
+    others = range(1, members)
+
     me = lax.axis_index("lat")
+    mine_part = lax.axis_index("ens")
     core = me % 2
     side = (me // 2) % 2
     plane = me // 4
@@ -46,44 +51,55 @@
 
     def copy(src, dst, ssem, rsem, to):
         return pltpu.make_async_remote_copy(
-            src_ref=src, dst_ref=dst, send_sem=ssem, recv_sem=rsem, device_id={"lat": to}, device_id_type=MESH
+            src_ref=src, dst_ref=dst, send_sem=ssem, recv_sem=rsem, device_id=to, device_id_type=MESH
         )
 
-    other_side = index_of(plane, 1 - side, core)
-    other_core = index_of(plane, side, 1 - core)
+    def part_span(p):
+        return slice(p * part_width, min(nx, (p + 1) * part_width))
+
+    def part_size(p):
+        return part_span(p).stop - part_span(p).start
+
+    other_side = {"lat": index_of(plane, 1 - side, core)}
+    other_core = {"lat": index_of(plane, side, 1 - core)}
     above = (me + 1) % count
     below = (me + count - 1) % count
     planes = [(plane + d) % depths for d in range(1, depths)]
 
     barrier = pltpu.get_barrier_semaphore()
-    partners = [index_of(z, side, core) for z in planes] + [other_side, other_core, above, below]
+    partners = [{"lat": index_of(z, side, core)} for z in planes]
+    partners += [other_side, other_core, {"lat": above}, {"lat": below}]
+    partners += [{"ens": (mine_part + d) % members} for d in others]
     for partner in partners:
-        pl.semaphore_signal(barrier, inc=1, device_id={"lat": partner}, device_id_type=MESH)
+        pl.semaphore_signal(barrier, inc=1, device_id=partner, device_id_type=MESH)
 
     wet_own = ocean_ref[...].astype(jnp.float32)
-    gathered[0, me] = depth_ref[...]
-    gathered[1, me] = wet_own
-    gathered[2, me] = mass_ref[...]
-    gathered[3, me] = wet_own * surf_in[...]
+    for p in range(members):
+        shared[0, me, p, :, 0:part_size(p)] = depth_ref[:, part_span(p)]
+        shared[1, me, p, :, 0:part_size(p)] = wet_own[:, part_span(p)]
+        shared[2, me, p, :, 0:part_size(p)] = mass_ref[:, part_span(p)]
+    right[me] = wet_own * surf_in[...]
     pl.semaphore_wait(barrier, len(partners))
 
     sent = []
 
-    def send(field, src_index, ssem, rsem, to):
-        part = gathered.at[field, src_index]
-        c = copy(part, part, ssem, rsem, to)
+    def block_of(f, index, part):
+        return shared.at[f, index, part] if f < 3 else right.at[index]
+
+    def send(ref, ssem, rsem, to):
+        c = copy(ref, ref, ssem, rsem, to)
         c.start()
         sent.append(c)
 
-    def arrived(field, src_index, ssem, rsem):
-        part = gathered.at[field, src_index]
-        copy(part, part, ssem, rsem, other_core).wait_recv()
+    def arrived(ref, ssem, rsem):
+        copy(ref, ref, ssem, rsem, other_core).wait_recv()
 
     for f in range(4):
+        own_block = block_of(f, me, mine_part)
         for z in planes:
-            send(f, me, zs.at[f, z], zr.at[f, plane], index_of(z, side, core))
-        send(f, me, ys.at[f, plane], yr.at[f, plane], other_side)
-        send(f, me, cs.at[f, plane], cr.at[f, plane], other_core)
+            send(own_block, zs.at[f, z], zr.at[f, plane], {"lat": index_of(z, side, core)})
+        send(own_block, ys.at[f, plane], yr.at[f, plane], other_side)
+        send(shared.at[f, me] if f < 3 else own_block, os.at[f], orx.at[f], other_core)
 
     for v in range(variables):
         for k in range(levels):
@@ -111,34 +127,61 @@
         ref[:, :, (tiles - 1) * LANES:] = jnp.zeros((row_tiles + 2, ROWS, LANES), jnp.float32)
     xbuf[...] = jnp.zeros_like(xbuf)
 
+    def sources(c):
+        places = [(z, index_of(z, side, c)) for z in planes]
+        return places + [(depths + z, index_of(z, 1 - side, c)) for z in [plane] + planes]
+
+    def pass_on(f, k, source):
+        ref = block_of(f, source, mine_part)
+        send(ref, cs.at[f, k], cr.at[f, k], other_core)
+        if f < 3:
+            for d in others:
+                send(ref, xs.at[f, d, k], xr.at[f, d, k], {"ens": (mine_part + d) % members})
+
     def from_planes(f):
         for z in planes:
             source = index_of(z, side, core)
-            arrived(f, source, zs.at[f, z], zr.at[f, z])
-            send(f, source, ys.at[f, z], yr.at[f, z], other_side)
-            send(f, source, cs.at[f, z], cr.at[f, z], other_core)
+            ref = block_of(f, source, mine_part)
+            arrived(ref, zs.at[f, z], zr.at[f, z])
+            send(ref, ys.at[f, z], yr.at[f, z], other_side)
+            pass_on(f, z, source)
 
     def from_side(f):
         for z in [plane] + planes:
             source = index_of(z, 1 - side, core)
-            arrived(f, source, ys.at[f, z], yr.at[f, z])
-            send(f, source, cs.at[f, depths + z], cr.at[f, depths + z], other_core)
+            arrived(block_of(f, source, mine_part), ys.at[f, z], yr.at[f, z])
+            pass_on(f, depths + z, source)
+
+    def from_members(f):
+        for k, source in sources(core):
+            for d in others:
+                ref = shared.at[f, source, (mine_part + members - d) % members]
+                arrived(ref, xs.at[f, d, k], xr.at[f, d, k])
+                send(ref, fs.at[f, d, k], fr.at[f, d, k], other_core)
 
     def from_core(f):
-        for z in [plane] + planes:
-            arrived(f, index_of(z, side, 1 - core), cs.at[f, z], cr.at[f, z])
-            arrived(f, index_of(z, 1 - side, 1 - core), cs.at[f, depths + z], cr.at[f, depths + z])
-
-    halo_up = copy(up_out, up_in, hs.at[0], hr.at[0], above)
-    halo_down = copy(down_out, down_in, hs.at[1], hr.at[1], below)
+        neighbour = index_of(plane, side, 1 - core)
+        arrived(shared.at[f, neighbour] if f < 3 else right.at[neighbour], os.at[f], orx.at[f])
+        for k, source in sources(1 - core):
+            arrived(block_of(f, source, mine_part), cs.at[f, k], cr.at[f, k])
+            if f < 3:
+                for d in others:
+                    ref = shared.at[f, source, (mine_part + members - d) % members]
+                    arrived(ref, fs.at[f, d, k], fr.at[f, d, k])
+
+    halo_up = copy(up_out, up_in, hs.at[0], hr.at[0], {"lat": above})
+    halo_down = copy(down_out, down_in, hs.at[1], hr.at[1], {"lat": below})
 
     from_planes(0)
     from_planes(1)
     from_side(0)
     from_planes(2)
     from_side(1)
+    from_members(0)
     from_planes(3)
     from_side(2)
+    from_members(1)
+    from_side(3)
 
     lane = lax.broadcasted_iota(jnp.int32, (ROWS, LANES), 1)
     sub = lax.broadcasted_iota(jnp.int32, (ROWS, LANES), 0)
@@ -177,7 +220,12 @@
         for r in range(block):
             for field, ref in targets:
                 for c in range(tiles):
-                    parts = [gathered[field, s * strip + t, r:r + 1, span(c)] for s in range(ROWS)]
+                    wide = span(c).stop - span(c).start
+                    p, at = c // part_tiles, c % part_tiles * LANES
+                    if field < 3:
+                        parts = [shared[field, s * strip + t, p, r:r + 1, at:at + wide] for s in range(ROWS)]
+                    else:
+                        parts = [right[s * strip + t, r:r + 1, span(c)] for s in range(ROWS)]
                     ref[t * block + r + 1, :, span(c)] = jnp.concatenate(parts, axis=0)
         return carry
 
@@ -186,8 +234,8 @@
 
     from_core(0)
     place_all(0, pbuf)
+    from_members(2)
     from_core(1)
-    from_side(3)
     halo_up.start()
     halo_down.start()
     place_all(1, qbuf)
@@ -196,9 +244,11 @@
 
     for field, ref in ((0, dbuf), (1, wbuf)):
         ref[...] = jnp.zeros_like(ref)
-        ref[0:block, 0:nx] = gathered[field, me]
-        ref[block:block + 1, 0:nx] = gathered[field, above, 0:1]
-        ref[ROWS - 1:ROWS, 0:nx] = gathered[field, below, block - 1:block]
+        for p in range(members):
+            at, wide = part_span(p), part_size(p)
+            ref[0:block, at] = shared[field, me, p, :, 0:wide]
+            ref[block:block + 1, at] = shared[field, above, p, 0:1, 0:wide]
+            ref[ROWS - 1:ROWS, at] = shared[field, below, p, block - 1:block, 0:wide]
 
     def links(t, carry):
         for (c, de), (_, we) in zip(east(lambda c: pbuf[t, :, cols(c)]), east(lambda c: qbuf[t, :, cols(c)])):
@@ -391,7 +441,7 @@
 
 
 def solution(mesh):
-    count = mesh.shape["lat"]
+    members, count = mesh.shape["ens"], mesh.shape["lat"]
     in_specs = (
         P("ens", None, "lat", None),
         P(("ens", "lat"), None),
@@ -410,6 +460,7 @@
         width = -(-nx // LANES) * LANES
         row_tiles = count * block // ROWS
         depths = count // 4
+        part_width = -(-width // LANES // members) * LANES
         fields = variables * levels
         vmem = pl.BlockSpec(memory_space=pltpu.VMEM)
         smem = pl.BlockSpec(memory_space=pltpu.SMEM)
@@ -417,12 +468,13 @@
         ext = pltpu.VMEM((ROWS, width), f32)
         dma = pltpu.SemaphoreType.DMA
         return pl.pallas_call(
-            functools.partial(kernel, count, block, nx, variables, levels),
+            functools.partial(kernel, members, count, block, nx, variables, levels),
             out_shape=(jax.ShapeDtypeStruct(cot_next.shape, f32), jax.ShapeDtypeStruct(cot_surface.shape, f32)),
             in_specs=[vmem, vmem, vmem, vmem, smem, vmem, vmem, vmem, smem],
             out_specs=(vmem, vmem),
             scratch_shapes=[
-                pltpu.VMEM((4, count, block, nx), f32),
+                pltpu.VMEM((3, count, members, block, part_width), f32),
+                pltpu.VMEM((count, block, nx), f32),
                 *[pltpu.VMEM((row_tiles + 2, ROWS, width), f32) for _ in range(5)],
                 pltpu.VMEM((block + 2, ROWS, width), f32),
                 pltpu.VMEM((block + 2, ROWS, width), f32),
@@ -434,7 +486,8 @@
                 pltpu.VMEM((-(-fields // 8) * 8, width), f32),
                 *[pltpu.VMEM((fields + levels, nx), f32) for _ in range(4)],
                 dma((4, depths)), dma((4, depths)), dma((4, depths)), dma((4, depths)),
-                dma((4, 2 * depths)), dma((4, 2 * depths)), dma((2,)), dma((2,)),
+                dma((4, 2 * depths)), dma((4, 2 * depths)), dma((4,)), dma((4,)),
+                *[dma((3, members, 2 * depths)) for _ in range(4)], dma((2,)), dma((2,)),
             ],
             compiler_params=pltpu.CompilerParams(
                 collective_id=0, has_side_effects=True, vmem_limit_bytes=60 * 1024 * 1024

time: 92.7 us -> 79.7 us (0.86)
  the two profiles are of different devices: /device:TPU:11 before, /device:TPU:12 now
where the time goes in v3:
time: 79.7 us; the launch traced here: 79.5 us
  Pallas kernels  75.2 us (94%)
  local copies, waits for them, and re-layouts  3.7 us (5%)
    pallas_call x1, Pallas kernels, shards(): pl.pallas_call(functools.partial(kernel, members, count, block, nx, varia...  75.2 us
    unnamed x4, local copies, waits for them, and re-layouts  3.7 us

profile of v3, /device:TPU:12, one launch (start us, length us, event | category | flops | bytes accessed | tf_op | source)
XLA Modules:
  0.0 79.5 jit_solution(8358455000449356936)
XLA Ops:
  0.6 75.2 %shard_map.104 = (f32[3,10,4,4320]{3,2,1,0:T(4,128)}, f32[4,4320]{1,0:T(4,128)}) custom-call(f32[3,10,4,4320]{3,2,1,0:T(4,128)} %cot_ref.1, f32[4,4320]{1,0:T(4,128)} %surf_in.1, f32[5,4,4320]{2,1,0:T(4,128)} %stencil_ref.1, f32[9,4,4320]{2,1,0:T(4,128)} %mix_ref.1, f32[3,10]{1,0:T(4,128)} %weights_ref.1, f32[4,4320]{1,0:T(4,128)} %depth_ref.1, ...), custom_call_target="tpu_custom_call" | custom-call | tf_op jit(solution)/shard_map/pallas_call | solution.py:470
  75.8 0.0 copy-start
  75.8 3.1 %copy.13 = f32[3,10,4,4320]{3,2,1,0:T(4,128)} copy(f32[3,10,4,4320]{3,2,1,0:T(4,128)} %get-tuple-element.4) | data formatting | bytes 4147200
  78.9 0.0 copy-done
  78.9 0.6 copy.14
Async XLA Ops:
  75.8 3.1 %copy-start = (f32[4,4320]{1,0:T(4,128)S(1)}, f32[4,4320]{1,0:T(4,128)}, u32[]{:S(2)}) copy-start(f32[4,4320]{1,0:T(4,128)} %get-tuple-element.5) | copy-start | bytes 207364
